TPU v7x, 1024 devices: a whole 8x8x8 slice. The times are simulated.
1024 devices in a mesh: expert: 64 (over x, y), head: 16 (over z, core).
Axes of the slice: x: 8, y: 8, z: 8, core: 2. Of those that a mesh axis runs over, the one named last changes fastest.
Arguments:
- latent: bfloat16 [2048, 1024], P('expert'), may hold values from -6 to 6
- routes: int32 [2048, 22], P('expert'), may hold values from 0 to 255, all different within a row; in each aligned block of 32 rows (0 to 31, 32 to 63, ...) at most 4 rows name the same one
- gate_q: int32 [2048, 22], P('expert'), may hold values from 1 to 255
- up_weight: bfloat16 [256, 1024, 2048], P('expert', None, 'head'), may hold values from -0.1875 to 0.1875
- down_weight: bfloat16 [256, 2048, 1024], P('expert', 'head'), may hold values from -0.125 to 0.125
- out_weight: bfloat16 [1024, 4096], P(None, 'head'), may hold values from -0.1875 to 0.1875
- cotangent: bfloat16 [2048, 4096], P('expert', 'head'), may hold values from -6 to 6
Outputs:
- mixed: bfloat16 [2048, 4096], P('expert', 'head')
- grad_up: bfloat16 [256, 1024, 2048], P('expert', None, 'head')
Inputs may be any that keep to these rules, and one draw needn't show every extreme that they name: `routes`: each row names 22 different experts. In each aligned block of 32 rows (the tokens of one index of expert) no expert is named by more than 4 rows, a bound that some block reaches.
All inputs are finite; a program needn't handle non-finite values.
Results may differ from a plain program's by a relative error of at most 0.029.
Values may be sent and summed in bfloat16 or wider, within the bound.
No kernel may reach another device: no remote copies, remote signals or barrier semaphores. Data moves between devices by JAX's collectives and lax.ppermute only.
A program may use at most 64 MiB of HBM per device.

v0:
```python
import jax
import jax.numpy as jnp
from jax import lax
from jax.experimental import pallas as pl
from jax.experimental.pallas import tpu as pltpu
from jax.sharding import Mesh, PartitionSpec as P

F32 = jnp.float32
BF16 = jnp.bfloat16
HEAD = ("z", "core")
QUAD = 4
CHUNKS = 4
MOST = 4
ROWS = 2 * MOST
ANY = pl.BlockSpec(memory_space=pl.ANY)
VMEM = pl.BlockSpec(memory_space=pltpu.VMEM)
SMEM = pl.BlockSpec(memory_space=pltpu.SMEM)


def call(kernel, outs, *args, scalars=0, flops=0, in_hbm=(), out_hbm=(), scratch=()):
    single = not isinstance(outs, (list, tuple))
    moved = sum(a.size * a.dtype.itemsize for a in args)
    ins = [SMEM if i < scalars else ANY if i in in_hbm else VMEM for i in range(len(args))]
    places = [ANY if i in out_hbm else VMEM for i in range(1 if single else len(outs))]
    return pl.pallas_call(
        kernel,
        out_shape=outs,
        in_specs=ins,
        out_specs=places[0] if single else places,
        scratch_shapes=scratch,
        compiler_params=pltpu.CompilerParams(vmem_limit_bytes=40 * 2**20),
        cost_estimate=pl.CostEstimate(flops=flops, bytes_accessed=2 * moved, transcendentals=0),
    )(*args)


def shape(*dims, dtype=BF16):
    return jax.ShapeDtypeStruct(dims, dtype)


def dot(a, b, dims, precision=None):
    return lax.dot_general(a, b, (dims, ((), ())), precision=precision, preferred_element_type=F32)


def halves(me_ref, rows):
    half = rows.shape[1] // 2
    first = me_ref[0] % 2 == 0
    left, right = rows[:, :half], rows[:, half:]
    return jnp.where(first, left, right), jnp.where(first, right, left)


def joined(me_ref, own, other):
    first = me_ref[0] % 2 == 0
    own, other = own.astype(F32), other.astype(F32)
    return jnp.concatenate([jnp.where(first, own, other), jnp.where(first, other, own)], axis=1)


def back_kernel(me_ref, cot_ref, out_w_ref, keep_ref, give_ref):
    part = dot(cot_ref[...], out_w_ref[...], ((1,), (1,)))
    keep, give = halves(me_ref, part)
    keep_ref[...] = keep
    give_ref[...] = give.astype(BF16)


def spread_kernel(keep_ref, got_ref, o_ref):
    rows = (keep_ref[...] + got_ref[...].astype(F32)).astype(BF16)
    for z in range(o_ref.shape[0]):
        o_ref[z] = rows


def sum_kernel(i_ref, o_ref):
    o_ref[...] = jnp.sum(i_ref[...].astype(F32), axis=0).astype(BF16)


def send_kernel(me_ref, table_ref, latent_ref, own_ref, other_ref, send_ref, coef_ref, buf, sems):
    count = send_ref.shape[0]
    tokens = latent_ref.shape[0]
    top = table_ref.shape[0] // 2
    step = count // CHUNKS
    back = joined(me_ref, own_ref[...], other_ref[...]).astype(BF16)
    latent = latent_ref[...]
    total = jnp.zeros((1, tokens), jnp.int32)
    for k in range(top):
        total = total + table_ref[top + k : top + k + 1, :]
    earlier = lax.broadcasted_iota(jnp.int32, (tokens, tokens), 0)
    later = lax.broadcasted_iota(jnp.int32, (tokens, tokens), 1)
    before = jnp.where(earlier < later, 1.0, 0.0).astype(BF16)
    is_latent = lax.broadcasted_iota(jnp.int32, (step, 1), 0) % ROWS < MOST
    copies = []
    for i in range(CHUNKS):
        at = pl.ds(step * i, step)
        row = lax.broadcasted_iota(jnp.int32, (step, tokens), 0) + step * i
        expert = QUAD * (row // ROWS) + me_ref[0]
        score = jnp.zeros((step, tokens), jnp.int32)
        for k in range(top):
            q = table_ref[top + k : top + k + 1, :]
            score = score + jnp.where(table_ref[k : k + 1, :] == expert, q, 0)
        score = score.astype(F32)
        named = score > 0.0
        rank = dot(jnp.where(named, 1.0, 0.0).astype(BF16), before, ((1,), (0,)))
        here = named & (rank == (row % MOST).astype(F32))
        coef_ref[at, :] = jnp.where(here, score, 0.0).astype(BF16)
        pick = jnp.where(here, 1.0, 0.0).astype(BF16)
        gate = jnp.sum(jnp.where(here, score / total.astype(F32), 0.0), axis=1, keepdims=True)
        latent_rows = dot(pick, latent, ((1,), (0,)))
        back_rows = dot(pick, back, ((1,), (0,)))
        buf[at, :] = jnp.where(is_latent, latent_rows, gate * back_rows).astype(BF16)
        copies.append(pltpu.make_async_copy(buf.at[at, :], send_ref.at[at, :], sems.at[i]))
        copies[-1].start()
    for copy in copies:
        copy.wait()


def pack_kernel(me_ref, up_ref, down_ref, *outs):
    width, unit = up_ref.shape[1], up_ref.shape[2]
    for d, o_ref in enumerate(outs, 1):
        expert = me_ref[0] ^ d
        o_ref[0:width, :] = up_ref[expert]
        for b in range(width // unit):
            o_ref[width + unit * b : width + unit * (b + 1), :] = down_ref[
                expert, :, unit * b : unit * (b + 1)
            ]


def expert_kernel(me_ref, rows_hbm, up_hbm, down_hbm, *refs):
    packs, refs = refs[: QUAD - 1], refs[QUAD - 1 :]
    out_hbm, *grads_hbm = refs[: QUAD + 1]
    rows_ref, up_ref, down_ref, out_ref, grad_ref, sems = refs[QUAD + 1 :]
    width, unit = up_hbm.shape[1], up_hbm.shape[2]
    count = rows_hbm.shape[0]
    half = width // 2
    me = me_ref[0]
    copies = []

    def fetch(source, target):
        copies.append(pltpu.make_async_copy(source, target, sems.at[len(copies)]))
        copies[-1].start()
        return copies[-1]

    first = [fetch(rows_hbm, rows_ref), fetch(up_hbm.at[me], up_ref.at[:, 0:unit])]
    for d, p in enumerate(packs, 1):
        at = pl.ds(unit * d, unit)
        first.append(fetch(p.at[pl.ds(0, width), :], up_ref.at[:, at]))
    second = [fetch(down_hbm.at[me], down_ref.at[0:unit, :])]
    for d, p in enumerate(packs, 1):
        at = pl.ds(unit * d, unit)
        for b in range(width // unit):
            block = p.at[pl.ds(width + unit * b, unit), :]
            second.append(fetch(block, down_ref.at[at, pl.ds(unit * b, unit)]))

    is_latent = lax.broadcasted_iota(jnp.int32, (count, 1), 0) % ROWS < MOST
    for copy in first:
        copy.wait()
    rows = rows_ref[...]
    act = jnp.maximum(dot(rows, up_ref[...], ((1,), (0,))), 0.0)
    hidden = act * act
    hidden = jnp.where(is_latent, hidden, pltpu.roll(hidden, MOST, 0)).astype(BF16)
    for copy in second:
        copy.wait()
    left = dot(hidden, down_ref[:, :half], ((1,), (0,)))
    right = dot(hidden, down_ref[:, half:], ((1,), (0,)))
    out_ref[...] = jnp.where(is_latent, left, right).astype(BF16)
    results = [fetch(out_ref, out_hbm)]
    hidden_grad = pltpu.roll(dot(rows, down_ref[...], ((1,), (1,))), count - MOST, 0)
    pre_grad = jnp.where(is_latent, hidden_grad * 2.0 * act, 0.0).astype(BF16)
    grad_ref[...] = dot(rows, pre_grad, ((0,), (0,))).astype(BF16)
    for d, g in enumerate(grads_hbm):
        results.append(fetch(grad_ref.at[:, pl.ds(unit * d, unit)], g))
    for copy in results:
        copy.wait()


def combine_kernel(me_ref, rows_ref, coef_ref, gate_ref, keep_ref, give_ref):
    count = rows_ref.shape[0]
    is_left = lax.broadcasted_iota(jnp.int32, (count, 1), 0) % ROWS < MOST
    coef = coef_ref[...].astype(F32)
    left = jnp.where(is_left, coef, 0.0).astype(BF16)
    right = jnp.where(is_left, 0.0, coef).astype(BF16)
    rows = rows_ref[...]
    total = jnp.sum(gate_ref[...].astype(F32), axis=1, keepdims=True)
    parts = [dot(c, rows, ((0,), (0,))) / total for c in (left, right)]
    keep, give = halves(me_ref, jnp.concatenate(parts, axis=1))
    keep_ref[...] = keep
    give_ref[...] = give.astype(BF16)


def mixed_kernel(me_ref, own_ref, other_ref, out_w_ref, o_ref):
    combined = joined(me_ref, own_ref[...], other_ref[...]).astype(BF16)
    o_ref[...] = dot(combined, out_w_ref[...], ((1,), (0,))).astype(BF16)


def grad_kernel(me_ref, *refs):
    grads, o_ref = refs[:-1], refs[-1]
    for d, g_ref in enumerate(grads):
        o_ref[me_ref[0] ^ d] = g_ref[...]


def exchange(rows, axis):
    peers = lax.axis_size(axis)
    split = rows.reshape(peers, rows.shape[0] // peers, rows.shape[1])
    moved = lax.all_to_all(split, axis, split_axis=0, concat_axis=0, tiled=True)
    return moved.reshape(rows.shape)


def swap(array, distance, back=False):
    chips = lax.axis_size("z")
    pairs = []
    for z in range(chips):
        for core in range(2):
            to = (z + 2 * core - 1) % chips if distance > 1 else z
            pairs.append((2 * z + core, 2 * to + core ^ (distance % 2)))
    return lax.ppermute(array, HEAD, [(b, a) for a, b in pairs] if back else pairs)


def sum_over_head(keep, give):
    chips = lax.axis_size("z")
    spread = call(spread_kernel, shape(chips, *keep.shape), keep, swap(give, 1))
    moved = lax.all_to_all(spread, "z", split_axis=0, concat_axis=0, tiled=True)
    own = call(sum_kernel, shape(*keep.shape), moved)
    return own, swap(own, 1)


def per_device(latent, routes, gate_q, up_weight, down_weight, out_weight, cotangent):
    groups = lax.axis_size("expert")
    tokens, width = latent.shape
    unit = up_weight.shape[2]
    count = groups * ROWS
    half = shape(tokens, width // 2)
    half_wide = shape(tokens, width // 2, dtype=F32)
    me = (2 * (lax.axis_index("z") & 1) + lax.axis_index("core")).astype(jnp.int32).reshape(1)
    table = jnp.concatenate([routes, gate_q], axis=1).T

    packs = call(
        pack_kernel,
        [shape(2 * width, unit)] * (QUAD - 1),
        me, up_weight, down_weight, scalars=1,
    )
    packs = [swap(p, d) for d, p in enumerate(packs, 1)]

    back = call(
        back_kernel, [half_wide, half], me, cotangent, out_weight,
        scalars=1, flops=2 * tokens * width * cotangent.shape[1],
    )
    back = sum_over_head(*back)
    send, coef = call(
        send_kernel,
        [shape(count, width), shape(count, tokens)],
        me, table, latent, *back,
        scalars=1, out_hbm=(0,),
        scratch=[pltpu.VMEM((count, width), BF16), pltpu.SemaphoreType.DMA((CHUNKS,))],
    )
    rows = exchange(send, "expert")
    hidden = unit * QUAD
    copies = 3 + 2 * QUAD + (QUAD - 1) * (width // unit)
    out, *grads = call(
        expert_kernel,
        [shape(count, width // 2)] + [shape(width, unit)] * QUAD,
        me, rows, up_weight, down_weight, *packs,
        scalars=1, flops=8 * count * width * hidden,
        in_hbm=range(1, 4 + QUAD), out_hbm=range(QUAD + 1),
        scratch=[
            pltpu.VMEM((count, width), BF16),
            pltpu.VMEM((width, hidden), BF16),
            pltpu.VMEM((hidden, width), BF16),
            pltpu.VMEM((count, width // 2), BF16),
            pltpu.VMEM((width, hidden), BF16),
            pltpu.SemaphoreType.DMA((copies,)),
        ],
    )
    grads = [grads[0]] + [swap(g, d, back=True) for d, g in enumerate(grads[1:], 1)]
    returned = exchange(out, "expert")
    comb = call(combine_kernel, [half_wide, half], me, returned, coef, gate_q, scalars=1)
    comb = sum_over_head(*comb)
    mixed = call(
        mixed_kernel, shape(tokens, out_weight.shape[1]), me, *comb, out_weight,
        scalars=1, flops=2 * tokens * width * out_weight.shape[1],
    )
    grad_up = call(grad_kernel, shape(*up_weight.shape), me, *grads, scalars=1)
    return (mixed, grad_up)


def solution(mesh):
    groups, members = mesh.devices.shape
    fine = Mesh(mesh.devices.reshape(groups, members // 2, 2), ("expert", *HEAD))
    placed = (
        P("expert", None),
        P("expert", None),
        P("expert", None),
        P("expert", None, HEAD),
        P("expert", HEAD, None),
        P(None, HEAD),
        P("expert", HEAD),
    )
    return jax.shard_map(
        per_device,
        mesh=fine,
        in_specs=placed,
        out_specs=(P("expert", HEAD), P("expert", None, HEAD)),
        check_vma=False,
    )
```

profile of v0, /device:TPU:1, one launch (start us, length us, event | category | flops | bytes accessed | tf_op | source)
XLA Modules:
  0.0 146.0 jit_solution(2456612391698633407)
XLA Ops:
  0.6 0.7 copy-done.7
  1.4 1.0 copy-done
  2.4 0.2 shard_map.86
  2.6 16.1 %collective-permute-start = (bf16[32,512]{1,0:T(8,128)(2,1)S(1)}, bf16[32,512]{1,0:T(8,128)(2,1)S(1)}, u32[]{:S(2)}, u32[]{:S(2)}) collective-permute-start(bf16[32,512]{1,0:T(8,128)(2,1)S(1)} %get-tuple-element.17), channel_id=1, source_target_pairs={{0,1},{1,0},{2,3},{3,2},{4,5},{5,4},{6,7},{7,6},{8,9},{9,8},{10,11... | collective-permute-start | bytes 98312 | tf_op jit(solution)/shard_map/ppermute | solution.py:211
  18.7 0.8 collective-permute-done.got_ref
  19.6 14.7 %all_to_all.20.i_ref = bf16[8,32,512]{2,1,0:T(8,128)(2,1)S(1)} all-to-all(bf16[8,32,512]{2,1,0:T(8,128)(2,1)S(1)} %shard_map.87), channel_id=1, replica_groups=mesh['expert'=64,'z'=8,'core'=2] {'z'}, dimensions={0} | all-to-all | bytes 524288 | tf_op jit(solution)/shard_map/all_to_all | solution.py:217
  34.4 3.7 %collective-permute-start.1 = (bf16[32,512]{1,0:T(8,128)(2,1)S(1)}, bf16[32,512]{1,0:T(8,128)(2,1)S(1)}, u32[]{:S(2)}, u32[]{:S(2)}) collective-permute-start(bf16[32,512]{1,0:T(8,128)(2,1)S(1)} %shard_map.88.own_ref), channel_id=1, source_target_pairs={{0,1},{1,0},{2,3},{3,2},{4,5},{5,4},{6,7},{7,6},{8,9},{9,8},{10,11... | collective-permute-start | bytes 98312 | tf_op jit(solution)/shard_map/ppermute | solution.py:211
  38.1 0.8 collective-permute-done.1.other_ref
  38.9 2.2 %shard_map.89 = (bf16[512,1024]{1,0:T(8,128)(2,1)S(1)}, bf16[512,32]{1,0:T(8,128)(2,1)S(1)}) custom-call(s32[1]{0:T(128)} %bitcast.me_ref, s32[44,32]{1,0:T(8,128)S(1)} %add_bitcast_fusion.table_ref, bf16[32,1024]{1,0:T(8,128)(2,1)S(1)} %copy-done.6, bf16[32,512]{1,0:T(8,128)(2,1)S(1)} %shard_map.88.own_ref, bf16[32,512]{1,0:T(8,128)(2,1)S(1)} %collective-permute-done.1.other_ref), custom_call_target="tpu_custom_call" | custom-call | bytes 273416 | tf_op jit(solution)/shard_map/pallas_call | solution.py:25
  41.1 0.0 copy-start.4
  41.2 1.0 copy-done.4
  42.1 13.3 %all-to-all-start.1 = ((bf16[64,8,1024]{2,1,0:T(8,128)(2,1)}), bf16[64,8,1024]{2,1,0:T(8,128)(2,1)S(1)}, u32[]{:S(2)}, u32[]{:S(2)}) async-start(bf16[64,8,1024]{2,1,0:T(8,128)(2,1)} %bitcast.9), calls=%async_computation.1 | async-start | bytes 2097152 | tf_op jit(solution)/shard_map/all_to_all | solution.py:200
  55.5 0.2 shard_map.90
  55.7 2.5 %collective-permute-start.2 = (bf16[2048,128]{1,0:T(8,128)(2,1)S(1)}, bf16[2048,128]{1,0:T(8,128)(2,1)S(1)}, u32[]{:S(2)}, u32[]{:S(2)}) collective-permute-start(bf16[2048,128]{1,0:T(8,128)(2,1)S(1)} %get-tuple-element.19), channel_id=1, source_target_pairs={{0,1},{1,0},{2,3},{3,2},{4,5},{5,4},{6,7},{7,6},{8,9},{9,8},{10,11... | collective-permute-start | bytes 1572872 | tf_op jit(solution)/shard_map/ppermute | solution.py:211
  58.2 2.2 %collective-permute-start.3 = (bf16[2048,128]{1,0:T(8,128)(2,1)S(1)}, bf16[2048,128]{1,0:T(8,128)(2,1)S(1)}, u32[]{:S(2)}, u32[]{:S(2)}) collective-permute-start(bf16[2048,128]{1,0:T(8,128)(2,1)S(1)} %get-tuple-element.20), channel_id=1, source_target_pairs={{0,14},{1,3},{2,0},{3,5},{4,2},{5,7},{6,4},{7,9},{8,6},{9,11},{10,... | collective-permute-start | bytes 1572872 | tf_op jit(solution)/shard_map/ppermute | solution.py:211
  60.4 3.3 %collective-permute-start.4 = (bf16[2048,128]{1,0:T(8,128)(2,1)S(1)}, bf16[2048,128]{1,0:T(8,128)(2,1)S(1)}, u32[]{:S(2)}, u32[]{:S(2)}) collective-permute-start(bf16[2048,128]{1,0:T(8,128)(2,1)S(1)} %get-tuple-element.21), channel_id=1, source_target_pairs={{0,15},{1,2},{2,1},{3,4},{4,3},{5,6},{6,5},{7,8},{8,7},{9,10},{10,... | collective-permute-start | bytes 1572872 | tf_op jit(solution)/shard_map/ppermute | solution.py:211
  63.7 0.8 copy-done.8
  64.5 5.2 %collective-permute-done.3.refs_1_ = bf16[2048,128]{1,0:T(8,128)(2,1)S(1)} collective-permute-done((bf16[2048,128]{1,0:T(8,128)(2,1)S(1)}, bf16[2048,128]{1,0:T(8,128)(2,1)S(1)}, u32[]{:S(2)}, u32[]{:S(2)}) %collective-permute-start.3) | collective-permute-done | bytes 524320 | tf_op jit(solution)/shard_map/ppermute | solution.py:211
  69.7 0.8 copy-done.10
  70.5 4.0 %collective-permute-done.4.refs_2_ = bf16[2048,128]{1,0:T(8,128)(2,1)S(1)} collective-permute-done((bf16[2048,128]{1,0:T(8,128)(2,1)S(1)}, bf16[2048,128]{1,0:T(8,128)(2,1)S(1)}, u32[]{:S(2)}, u32[]{:S(2)}) %collective-permute-start.4) | collective-permute-done | bytes 524320 | tf_op jit(solution)/shard_map/ppermute | solution.py:211
  74.5 0.8 copy-done.12
  75.3 7.2 %all-to-all-done.1 = bf16[64,8,1024]{2,1,0:T(8,128)(2,1)S(1)} async-done(((bf16[64,8,1024]{2,1,0:T(8,128)(2,1)}), bf16[64,8,1024]{2,1,0:T(8,128)(2,1)S(1)}, u32[]{:S(2)}, u32[]{:S(2)}) %all-to-all-start.1) | async-done | bytes 1048608 | tf_op jit(solution)/shard_map/all_to_all | solution.py:200
  82.5 1.0 copy-done.9
  83.5 1.0 copy-done.11
  84.6 1.0 copy-done.13
  85.6 4.1 %shard_map.91 = (bf16[512,512]{1,0:T(8,128)(2,1)S(1)}, bf16[1024,128]{1,0:T(8,128)(2,1)S(1)}, bf16[1024,128]{1,0:T(8,128)(2,1)S(1)}, bf16[1024,128]{1,0:T(8,128)(2,1)S(1)}, bf16[1024,128]{1,0:T(8,128)(2,1)S(1)}) custom-call(s32[1]{0:T(128)} %bitcast.me_ref, bf16[512,1024]{1,0:T(8,128)(2,1)S(1)} %bitcast.8, bf16[4,1024,128]{2,1,0:T(8,128)(2,1)S(1)} %copy-done.2, ...), custom_call_target="tpu_custom_call" | custom-call | flops 2147483648 | bytes 9437192 | tf_op jit(solution)/shard_map/pallas_call | solution.py:25
  89.7 0.0 copy-start.5
  89.7 0.8 copy-done.5
  90.5 0.7 copy-done.14
  91.2 0.7 copy-done.16
  91.9 0.7 copy-done.18
  92.6 8.8 %all-to-all-start.2 = ((bf16[64,8,512]{2,1,0:T(8,128)(2,1)}), bf16[64,8,512]{2,1,0:T(8,128)(2,1)S(1)}, u32[]{:S(2)}, u32[]{:S(2)}) async-start(bf16[64,8,512]{2,1,0:T(8,128)(2,1)} %bitcast.10), calls=%async_computation.2 | async-start | bytes 1048576 | tf_op jit(solution)/shard_map/all_to_all | solution.py:200
  101.4 0.1 copy.9.gate_ref
  101.5 15.9 %all-to-all-done.2 = bf16[64,8,512]{2,1,0:T(8,128)(2,1)S(1)} async-done(((bf16[64,8,512]{2,1,0:T(8,128)(2,1)}), bf16[64,8,512]{2,1,0:T(8,128)(2,1)S(1)}, u32[]{:S(2)}, u32[]{:S(2)}) %all-to-all-start.2) | async-done | bytes 524320 | tf_op jit(solution)/shard_map/all_to_all | solution.py:200
  117.4 0.3 shard_map.92
  117.7 6.1 %collective-permute-start.5 = (bf16[32,512]{1,0:T(8,128)(2,1)S(1)}, bf16[32,512]{1,0:T(8,128)(2,1)S(1)}, u32[]{:S(2)}, u32[]{:S(2)}) collective-permute-start(bf16[32,512]{1,0:T(8,128)(2,1)S(1)} %get-tuple-element.25), channel_id=1, source_target_pairs={{0,1},{1,0},{2,3},{3,2},{4,5},{5,4},{6,7},{7,6},{8,9},{9,8},{10,11... | collective-permute-start | bytes 98312 | tf_op jit(solution)/shard_map/ppermute | solution.py:211
  123.8 0.8 collective-permute-done.5.got_ref
  124.7 0.7 shard_map.93
  125.4 3.5 %all-to-all-start.3 = ((bf16[8,32,512]{2,1,0:T(8,128)(2,1)}), bf16[8,32,512]{2,1,0:T(8,128)(2,1)S(1)}, u32[]{:S(2)}, u32[]{:S(2)}) async-start(bf16[8,32,512]{2,1,0:T(8,128)(2,1)} %shard_map.93), calls=%async_computation.3 | async-start | bytes 524288 | tf_op jit(solution)/shard_map/all_to_all | solution.py:217
  129.0 2.3 %collective-permute-start.7 = (bf16[1024,128]{1,0:T(8,128)(2,1)S(1)}, bf16[1024,128]{1,0:T(8,128)(2,1)S(1)}, u32[]{:S(2)}, u32[]{:S(2)}) collective-permute-start(bf16[1024,128]{1,0:T(8,128)(2,1)S(1)} %copy-done.19), channel_id=1, source_target_pairs={{1,0},{0,1},{3,2},{2,3},{5,4},{4,5},{7,6},{6,7},{9,8},{8,9},{11,10... | collective-permute-start | bytes 786440 | tf_op jit(solution)/shard_map/ppermute | solution.py:211
  131.2 4.8 %collective-permute-start.8 = (bf16[1024,128]{1,0:T(8,128)(2,1)S(1)}, bf16[1024,128]{1,0:T(8,128)(2,1)S(1)}, u32[]{:S(2)}, u32[]{:S(2)}) collective-permute-start(bf16[1024,128]{1,0:T(8,128)(2,1)S(1)} %copy-done.17), channel_id=1, source_target_pairs={{14,0},{3,1},{0,2},{5,3},{2,4},{7,5},{4,6},{9,7},{6,8},{11,9},{8,1... | collective-permute-start | bytes 786440 | tf_op jit(solution)/shard_map/ppermute | solution.py:211
  136.0 2.0 %collective-permute-start.9 = (bf16[1024,128]{1,0:T(8,128)(2,1)S(1)}, bf16[1024,128]{1,0:T(8,128)(2,1)S(1)}, u32[]{:S(2)}, u32[]{:S(2)}) collective-permute-start(bf16[1024,128]{1,0:T(8,128)(2,1)S(1)} %copy-done.15), channel_id=1, source_target_pairs={{15,0},{2,1},{1,2},{4,3},{3,4},{6,5},{5,6},{8,7},{7,8},{10,9},{9,1... | collective-permute-start | bytes 786440 | tf_op jit(solution)/shard_map/ppermute | solution.py:211
  138.1 3.2 %all-to-all-done.3.i_ref = bf16[8,32,512]{2,1,0:T(8,128)(2,1)S(1)} async-done(((bf16[8,32,512]{2,1,0:T(8,128)(2,1)}), bf16[8,32,512]{2,1,0:T(8,128)(2,1)S(1)}, u32[]{:S(2)}, u32[]{:S(2)}) %all-to-all-start.3) | async-done | bytes 262176 | tf_op jit(solution)/shard_map/all_to_all | solution.py:217
  141.3 2.5 %collective-permute-start.6 = (bf16[32,512]{1,0:T(8,128)(2,1)S(1)}, bf16[32,512]{1,0:T(8,128)(2,1)S(1)}, u32[]{:S(2)}, u32[]{:S(2)}) collective-permute-start(bf16[32,512]{1,0:T(8,128)(2,1)S(1)} %shard_map.94.own_ref), channel_id=1, source_target_pairs={{0,1},{1,0},{2,3},{3,2},{4,5},{5,4},{6,7},{7,6},{8,9},{9,8},{10,11... | collective-permute-start | bytes 98312 | tf_op jit(solution)/shard_map/ppermute | solution.py:211
  143.7 0.3 collective-permute-done.9.refs_3_
  144.0 1.0 shard_map.96
  145.1 0.2 copy-done.1
  145.2 0.8 shard_map.95
  (36 shorter events, 0.2 us)
Async XLA Ops:
  0.6 0.7 copy-start.7
  1.3 1.0 copy-start
  2.6 16.9 %collective-permute-start = (bf16[32,512]{1,0:T(8,128)(2,1)S(1)}, bf16[32,512]{1,0:T(8,128)(2,1)S(1)}, u32[]{:S(2)}, u32[]{:S(2)}) collective-permute-start(bf16[32,512]{1,0:T(8,128)(2,1)S(1)} %get-tuple-element.17), channel_id=1, source_target_pairs={{0,1},{1,0},{2,3},{3,2},{4,5},{5,4},{6,7},{7,6},{8,9},{9,8},{10,11... | collective-permute-start | bytes 98312 | tf_op jit(solution)/shard_map/ppermute | solution.py:211
  34.3 3.7 %copy-start.20 = (s32[32,22]{0,1:T(8,128)S(1)}, s32[32,22]{0,1:T(8,128)}, u32[]{:S(2)}) copy-start(s32[32,22]{0,1:T(8,128)} %param.9) | copy-start | bytes 8452
  34.3 3.8 %copy-start.21 = (s32[32,22]{0,1:T(8,128)S(1)}, s32[32,22]{0,1:T(8,128)}, u32[]{:S(2)}) copy-start(s32[32,22]{0,1:T(8,128)} %param.8) | copy-start | bytes 8452
  34.3 4.6 %copy-start.6 = (bf16[32,1024]{1,0:T(8,128)(2,1)S(1)}, bf16[32,1024]{1,0:T(8,128)(2,1)}, u32[]{:S(2)}) copy-start(bf16[32,1024]{1,0:T(8,128)(2,1)} %latent_ref.1) | copy-start | bytes 196612
  34.4 4.5 %collective-permute-start.1 = (bf16[32,512]{1,0:T(8,128)(2,1)S(1)}, bf16[32,512]{1,0:T(8,128)(2,1)S(1)}, u32[]{:S(2)}, u32[]{:S(2)}) collective-permute-start(bf16[32,512]{1,0:T(8,128)(2,1)S(1)} %shard_map.88.own_ref), channel_id=1, source_target_pairs={{0,1},{1,0},{2,3},{3,2},{4,5},{5,4},{6,7},{7,6},{8,9},{9,8},{10,11... | collective-permute-start | bytes 98312 | tf_op jit(solution)/shard_map/ppermute | solution.py:211
  41.1 1.0 copy-start.4
  42.1 13.3 %copy-start.2 = (bf16[4,1024,128]{2,1,0:T(8,128)(2,1)S(1)}, bf16[4,1024,128]{2,1,0:T(8,128)(2,1)}, u32[]{:S(2)}) copy-start(bf16[4,1024,128]{2,1,0:T(8,128)(2,1)} %up_hbm.1) | copy-start | bytes 3145732
  42.1 13.4 %copy-start.3 = (bf16[4,128,1024]{2,1,0:T(8,128)(2,1)S(1)}, bf16[4,128,1024]{2,1,0:T(8,128)(2,1)}, u32[]{:S(2)}) copy-start(bf16[4,128,1024]{2,1,0:T(8,128)(2,1)} %down_hbm.1) | copy-start | bytes 3145732
  42.1 40.4 %all-to-all-start.1 = ((bf16[64,8,1024]{2,1,0:T(8,128)(2,1)}), bf16[64,8,1024]{2,1,0:T(8,128)(2,1)S(1)}, u32[]{:S(2)}, u32[]{:S(2)}) async-start(bf16[64,8,1024]{2,1,0:T(8,128)(2,1)} %bitcast.9), calls=%async_computation.1 | async-start | bytes 2097152 | tf_op jit(solution)/shard_map/all_to_all | solution.py:200
  55.7 8.0 %collective-permute-start.2 = (bf16[2048,128]{1,0:T(8,128)(2,1)S(1)}, bf16[2048,128]{1,0:T(8,128)(2,1)S(1)}, u32[]{:S(2)}, u32[]{:S(2)}) collective-permute-start(bf16[2048,128]{1,0:T(8,128)(2,1)S(1)} %get-tuple-element.19), channel_id=1, source_target_pairs={{0,1},{1,0},{2,3},{3,2},{4,5},{5,4},{6,7},{7,6},{8,9},{9,8},{10,11... | collective-permute-start | bytes 1572872 | tf_op jit(solution)/shard_map/ppermute | solution.py:211
  58.2 11.4 %collective-permute-start.3 = (bf16[2048,128]{1,0:T(8,128)(2,1)S(1)}, bf16[2048,128]{1,0:T(8,128)(2,1)S(1)}, u32[]{:S(2)}, u32[]{:S(2)}) collective-permute-start(bf16[2048,128]{1,0:T(8,128)(2,1)S(1)} %get-tuple-element.20), channel_id=1, source_target_pairs={{0,14},{1,3},{2,0},{3,5},{4,2},{5,7},{6,4},{7,9},{8,6},{9,11},{10,... | collective-permute-start | bytes 1572872 | tf_op jit(solution)/shard_map/ppermute | solution.py:211
  60.4 14.1 %collective-permute-start.4 = (bf16[2048,128]{1,0:T(8,128)(2,1)S(1)}, bf16[2048,128]{1,0:T(8,128)(2,1)S(1)}, u32[]{:S(2)}, u32[]{:S(2)}) collective-permute-start(bf16[2048,128]{1,0:T(8,128)(2,1)S(1)} %get-tuple-element.21), channel_id=1, source_target_pairs={{0,15},{1,2},{2,1},{3,4},{4,3},{5,6},{6,5},{7,8},{8,7},{9,10},{10,... | collective-permute-start | bytes 1572872 | tf_op jit(solution)/shard_map/ppermute | solution.py:211
  63.7 0.8 copy-start.8
  69.7 0.8 copy-start.10
  74.5 0.8 copy-start.12
  82.5 1.0 copy-start.9
  83.5 1.0 copy-start.11
  84.6 1.0 copy-start.13
  89.7 0.8 copy-start.5
  90.5 0.7 copy-start.14
  91.2 0.7 copy-start.16
  91.9 0.7 copy-start.18
  92.6 24.8 %all-to-all-start.2 = ((bf16[64,8,512]{2,1,0:T(8,128)(2,1)}), bf16[64,8,512]{2,1,0:T(8,128)(2,1)S(1)}, u32[]{:S(2)}, u32[]{:S(2)}) async-start(bf16[64,8,512]{2,1,0:T(8,128)(2,1)} %bitcast.10), calls=%async_computation.2 | async-start | bytes 1048576 | tf_op jit(solution)/shard_map/all_to_all | solution.py:200
  117.7 7.0 %collective-permute-start.5 = (bf16[32,512]{1,0:T(8,128)(2,1)S(1)}, bf16[32,512]{1,0:T(8,128)(2,1)S(1)}, u32[]{:S(2)}, u32[]{:S(2)}) collective-permute-start(bf16[32,512]{1,0:T(8,128)(2,1)S(1)} %get-tuple-element.25), channel_id=1, source_target_pairs={{0,1},{1,0},{2,3},{3,2},{4,5},{5,4},{6,7},{7,6},{8,9},{9,8},{10,11... | collective-permute-start | bytes 98312 | tf_op jit(solution)/shard_map/ppermute | solution.py:211
  124.7 4.3 %copy-start.19 = (bf16[1024,128]{1,0:T(8,128)(2,1)S(1)}, bf16[1024,128]{1,0:T(8,128)(2,1)}, u32[]{:S(2)}) copy-start(bf16[1024,128]{1,0:T(8,128)(2,1)} %copy-done.18) | copy-start | bytes 786436
  125.4 5.8 %copy-start.17 = (bf16[1024,128]{1,0:T(8,128)(2,1)S(1)}, bf16[1024,128]{1,0:T(8,128)(2,1)}, u32[]{:S(2)}) copy-start(bf16[1024,128]{1,0:T(8,128)(2,1)} %copy-done.16) | copy-start | bytes 786436
  125.4 10.6 %copy-start.15 = (bf16[1024,128]{1,0:T(8,128)(2,1)S(1)}, bf16[1024,128]{1,0:T(8,128)(2,1)}, u32[]{:S(2)}) copy-start(bf16[1024,128]{1,0:T(8,128)(2,1)} %copy-done.14) | copy-start | bytes 786436
  125.4 15.8 %all-to-all-start.3 = ((bf16[8,32,512]{2,1,0:T(8,128)(2,1)}), bf16[8,32,512]{2,1,0:T(8,128)(2,1)S(1)}, u32[]{:S(2)}, u32[]{:S(2)}) async-start(bf16[8,32,512]{2,1,0:T(8,128)(2,1)} %shard_map.93), calls=%async_computation.3 | async-start | bytes 524288 | tf_op jit(solution)/shard_map/all_to_all | solution.py:217
  129.0 14.8 %collective-permute-start.7 = (bf16[1024,128]{1,0:T(8,128)(2,1)S(1)}, bf16[1024,128]{1,0:T(8,128)(2,1)S(1)}, u32[]{:S(2)}, u32[]{:S(2)}) collective-permute-start(bf16[1024,128]{1,0:T(8,128)(2,1)S(1)} %copy-done.19), channel_id=1, source_target_pairs={{1,0},{0,1},{3,2},{2,3},{5,4},{4,5},{7,6},{6,7},{9,8},{8,9},{11,10... | collective-permute-start | bytes 786440 | tf_op jit(solution)/shard_map/ppermute | solution.py:211
  131.2 12.5 %collective-permute-start.8 = (bf16[1024,128]{1,0:T(8,128)(2,1)S(1)}, bf16[1024,128]{1,0:T(8,128)(2,1)S(1)}, u32[]{:S(2)}, u32[]{:S(2)}) collective-permute-start(bf16[1024,128]{1,0:T(8,128)(2,1)S(1)} %copy-done.17), channel_id=1, source_target_pairs={{14,0},{3,1},{0,2},{5,3},{2,4},{7,5},{4,6},{9,7},{6,8},{11,9},{8,1... | collective-permute-start | bytes 786440 | tf_op jit(solution)/shard_map/ppermute | solution.py:211
  136.0 8.0 %collective-permute-start.9 = (bf16[1024,128]{1,0:T(8,128)(2,1)S(1)}, bf16[1024,128]{1,0:T(8,128)(2,1)S(1)}, u32[]{:S(2)}, u32[]{:S(2)}) collective-permute-start(bf16[1024,128]{1,0:T(8,128)(2,1)S(1)} %copy-done.15), channel_id=1, source_target_pairs={{15,0},{2,1},{1,2},{4,3},{3,4},{6,5},{5,6},{8,7},{7,8},{10,9},{9,1... | collective-permute-start | bytes 786440 | tf_op jit(solution)/shard_map/ppermute | solution.py:211
  141.3 3.8 %collective-permute-start.6 = (bf16[32,512]{1,0:T(8,128)(2,1)S(1)}, bf16[32,512]{1,0:T(8,128)(2,1)S(1)}, u32[]{:S(2)}, u32[]{:S(2)}) collective-permute-start(bf16[32,512]{1,0:T(8,128)(2,1)S(1)} %shard_map.94.own_ref), channel_id=1, source_target_pairs={{0,1},{1,0},{2,3},{3,2},{4,5},{5,4},{6,7},{7,6},{8,9},{9,8},{10,11... | collective-permute-start | bytes 98312 | tf_op jit(solution)/shard_map/ppermute | solution.py:211
  144.0 1.2 copy-start.1
where the time goes:
time: 147 us; the launch traced here: 146 us
  starting transfers between devices  71.1 us (48%)
  waiting for transfers between devices  38.2 us (26%)
  blocking collectives  14.7 us (10%)
  local copies, waits for them, and re-layouts  11.4 us (8%)
  Pallas kernels  9.7 us (7%)
    ppermute x10, starting transfers between devices, swap(): lax.ppermute(array, HEAD, [(b, a) for a, b in pairs] if back else pairs)  45.4 us
    all_to_all x2, waiting for transfers between devices, exchange(): moved = lax.all_to_all(split, axis, split_axis=0, concat_axis=0, tiled=True)  23.1 us
    all_to_all x2, starting transfers between devices, exchange(): moved = lax.all_to_all(split, axis, split_axis=0, concat_axis=0, tiled=True)  22.1 us
    all_to_all x1, blocking collectives, sum_over_head(): moved = lax.all_to_all(spread, 'z', split_axis=0, concat_axis=0, tiled=True)  14.7 us
    ppermute x10, waiting for transfers between devices, swap(): lax.ppermute(array, HEAD, [(b, a) for a, b in pairs] if back else pairs)  12 us
    unnamed x45, local copies, waits for them, and re-layouts  11.4 us
    pallas_call x11, Pallas kernels, call(): pl.pallas_call(kernel, out_shape=outs, in_specs=ins, out_specs=places[0]...  9.7 us
    all_to_all x1, starting transfers between devices, sum_over_head(): moved = lax.all_to_all(spread, 'z', split_axis=0, concat_axis=0, tiled=True)  3.54 us
  transfers between devices with their start and end apart: 13, of which 9 were waited for; matrix products, arithmetic and copies ran while one was open for 0% of the time, Pallas kernels for 1%

commit v1 on v0

--- a/solution.py
+++ b/solution.py
@@ -10,6 +10,7 @@
 HEAD = ("z", "core")
 QUAD = 4
 CHUNKS = 4
+MIB = 2**20
 MOST = 4
 ROWS = 2 * MOST
 ANY = pl.BlockSpec(memory_space=pl.ANY)
@@ -17,7 +18,7 @@
 SMEM = pl.BlockSpec(memory_space=pltpu.SMEM)
 
 
-def call(kernel, outs, *args, scalars=0, flops=0, in_hbm=(), out_hbm=(), scratch=()):
+def call(kernel, outs, *args, scalars=0, flops=0, in_hbm=(), out_hbm=(), scratch=(), vmem=32):
     single = not isinstance(outs, (list, tuple))
     moved = sum(a.size * a.dtype.itemsize for a in args)
     ins = [SMEM if i < scalars else ANY if i in in_hbm else VMEM for i in range(len(args))]
@@ -28,7 +29,7 @@
         in_specs=ins,
         out_specs=places[0] if single else places,
         scratch_shapes=scratch,
-        compiler_params=pltpu.CompilerParams(vmem_limit_bytes=40 * 2**20),
+        compiler_params=pltpu.CompilerParams(vmem_limit_bytes=vmem * MIB),
         cost_estimate=pl.CostEstimate(flops=flops, bytes_accessed=2 * moved, transcendentals=0),
     )(*args)
 
@@ -54,7 +55,15 @@
     return jnp.concatenate([jnp.where(first, own, other), jnp.where(first, other, own)], axis=1)
 
 
-def back_kernel(me_ref, cot_ref, out_w_ref, keep_ref, give_ref):
+def back_kernel(me_ref, cot_hbm, out_w_hbm, keep_ref, give_ref, cot_ref, out_w_ref, sems):
+    copies = [
+        pltpu.make_async_copy(out_w_hbm, out_w_ref, sems.at[0]),
+        pltpu.make_async_copy(cot_hbm, cot_ref, sems.at[1]),
+    ]
+    for copy in copies:
+        copy.start()
+    for copy in copies:
+        copy.wait()
     part = dot(cot_ref[...], out_w_ref[...], ((1,), (1,)))
     keep, give = halves(me_ref, part)
     keep_ref[...] = keep
@@ -238,14 +247,19 @@
 
     back = call(
         back_kernel, [half_wide, half], me, cotangent, out_weight,
-        scalars=1, flops=2 * tokens * width * cotangent.shape[1],
+        scalars=1, flops=2 * tokens * width * cotangent.shape[1], in_hbm=(1, 2), vmem=53,
+        scratch=[
+            pltpu.VMEM(cotangent.shape, BF16),
+            pltpu.VMEM(out_weight.shape, BF16),
+            pltpu.SemaphoreType.DMA((2,)),
+        ],
     )
     back = sum_over_head(*back)
     send, coef = call(
         send_kernel,
         [shape(count, width), shape(count, tokens)],
         me, table, latent, *back,
-        scalars=1, out_hbm=(0,),
+        scalars=1, out_hbm=(0,), vmem=53,
         scratch=[pltpu.VMEM((count, width), BF16), pltpu.SemaphoreType.DMA((CHUNKS,))],
     )
     rows = exchange(send, "expert")
@@ -256,7 +270,7 @@
         [shape(count, width // 2)] + [shape(width, unit)] * QUAD,
         me, rows, up_weight, down_weight, *packs,
         scalars=1, flops=8 * count * width * hidden,
-        in_hbm=range(1, 4 + QUAD), out_hbm=range(QUAD + 1),
+        in_hbm=range(1, 4 + QUAD), out_hbm=range(QUAD + 1), vmem=49,
         scratch=[
             pltpu.VMEM((count, width), BF16),
             pltpu.VMEM((width, hidden), BF16),
@@ -267,14 +281,14 @@
         ],
     )
     grads = [grads[0]] + [swap(g, d, back=True) for d, g in enumerate(grads[1:], 1)]
-    returned = exchange(out, "expert")
+    grad_up = call(grad_kernel, shape(*up_weight.shape), me, *grads, scalars=1)
+    returned, grad_up = lax.optimization_barrier((exchange(out, "expert"), grad_up))
     comb = call(combine_kernel, [half_wide, half], me, returned, coef, gate_q, scalars=1)
     comb = sum_over_head(*comb)
     mixed = call(
         mixed_kernel, shape(tokens, out_weight.shape[1]), me, *comb, out_weight,
         scalars=1, flops=2 * tokens * width * out_weight.shape[1],
     )
-    grad_up = call(grad_kernel, shape(*up_weight.shape), me, *grads, scalars=1)
     return (mixed, grad_up)
 
 

time: 147 us -> 139 us (0.946)
  blocking collectives: 14.7 us -> 29.6 us
  local copies, waits for them, and re-layouts: 11.4 us -> 2.56 us
  waiting for transfers between devices: 38.2 us -> 29.5 us
  starting transfers between devices: 71.1 us -> 65.9 us
    all_to_all x1 -> x2, blocking collectives: 14.7 us -> 29.6 us  [sum_over_head(): moved = lax.all_to_all(spread, 'z', split_axis=0, concat_axis=0, tiled=True)]
    all_to_all x2, waiting for transfers between devices: 23.1 us -> 9.21 us  [exchange(): moved = lax.all_to_all(split, axis, split_axis=0, concat_axis=0, tiled=True)]
    unnamed x45 -> x21, local copies, waits for them, and re-layouts: 11.4 us -> 2.56 us
    ppermute x10, waiting for transfers between devices: 12 us -> 20.2 us  [swap(): lax.ppermute(array, HEAD, [(b, a) for a, b in pairs] if back else pairs)]
    all_to_all x1 -> x0, starting transfers between devices: 3.54 us -> none  [sum_over_head(): moved = lax.all_to_all(spread, 'z', split_axis=0, concat_axis=0, tiled=True)]
    all_to_all x1 -> x0, waiting for transfers between devices: 3.16 us -> none  [sum_over_head(): moved = lax.all_to_all(spread, 'z', split_axis=0, concat_axis=0, tiled=True)]
    ppermute x10, starting transfers between devices: 45.4 us -> 43.7 us  [swap(): lax.ppermute(array, HEAD, [(b, a) for a, b in pairs] if back else pairs)]
  transfers between devices with their start and end apart: 13 -> 12, of which waited for: 9 -> 10; matrix products, arithmetic and copies ran while one was open for 0% -> 0% of each run, Pallas kernels for 1% -> 1%
where the time goes in v1:
time: 139 us; the launch traced here: 138 us
  starting transfers between devices  65.9 us (47%)
  blocking collectives  29.6 us (21%)
  waiting for transfers between devices  29.5 us (21%)
  Pallas kernels  9.43 us (7%)
  local copies, waits for them, and re-layouts  2.56 us (2%)
    ppermute x10, starting transfers between devices, swap(): lax.ppermute(array, HEAD, [(b, a) for a, b in pairs] if back else pairs)  43.7 us
    all_to_all x2, blocking collectives, sum_over_head(): moved = lax.all_to_all(spread, 'z', split_axis=0, concat_axis=0, tiled=True)  29.6 us
    all_to_all x2, starting transfers between devices, exchange(): moved = lax.all_to_all(split, axis, split_axis=0, concat_axis=0, tiled=True)  22.2 us
    ppermute x10, waiting for transfers between devices, swap(): lax.ppermute(array, HEAD, [(b, a) for a, b in pairs] if back else pairs)  20.2 us
    pallas_call x11, Pallas kernels, call(): pl.pallas_call(kernel, out_shape=outs, in_specs=ins, out_specs=places[0]...  9.43 us
    all_to_all x2, waiting for transfers between devices, exchange(): moved = lax.all_to_all(split, axis, split_axis=0, concat_axis=0, tiled=True)  9.21 us
  transfers between devices with their start and end apart: 12, of which 10 were waited for; matrix products, arithmetic and copies ran while one was open for 0% of the time, Pallas kernels for 1%

profile of v1, /device:TPU:1, one launch (start us, length us, event | category | flops | bytes accessed | tf_op | source)
XLA Modules:
  0.0 137.9 jit_solution(8249298193288904486)
XLA Ops:
  0.6 0.0 copy-start.5
  0.6 0.7 copy-done.5
  1.4 1.0 copy-done
  2.4 0.3 shard_map.86
  2.7 16.1 %collective-permute-start = (bf16[32,512]{1,0:T(8,128)(2,1)S(1)}, bf16[32,512]{1,0:T(8,128)(2,1)S(1)}, u32[]{:S(2)}, u32[]{:S(2)}) collective-permute-start(bf16[32,512]{1,0:T(8,128)(2,1)S(1)} %get-tuple-element.19), channel_id=1, source_target_pairs={{0,1},{1,0},{2,3},{3,2},{4,5},{5,4},{6,7},{7,6},{8,9},{9,8},{10,11... | collective-permute-start | bytes 98312 | tf_op jit(solution)/shard_map/ppermute | solution.py:220
  18.8 0.8 collective-permute-done.got_ref
  19.7 14.7 %all_to_all.20.i_ref = bf16[8,32,512]{2,1,0:T(8,128)(2,1)S(1)} all-to-all(bf16[8,32,512]{2,1,0:T(8,128)(2,1)S(1)} %shard_map.87), channel_id=1, replica_groups=mesh['expert'=64,'z'=8,'core'=2] {'z'}, dimensions={0} | all-to-all | bytes 524288 | tf_op jit(solution)/shard_map/all_to_all | solution.py:226
  34.5 3.7 %collective-permute-start.1 = (bf16[32,512]{1,0:T(8,128)(2,1)S(1)}, bf16[32,512]{1,0:T(8,128)(2,1)S(1)}, u32[]{:S(2)}, u32[]{:S(2)}) collective-permute-start(bf16[32,512]{1,0:T(8,128)(2,1)S(1)} %shard_map.88.own_ref), channel_id=1, source_target_pairs={{0,1},{1,0},{2,3},{3,2},{4,5},{5,4},{6,7},{7,6},{8,9},{9,8},{10,11... | collective-permute-start | bytes 98312 | tf_op jit(solution)/shard_map/ppermute | solution.py:220
  38.2 0.0 copy-done.8
  38.2 0.0 copy-done.9
  38.2 0.8 collective-permute-done.1.other_ref
  39.0 0.0 copy-done.4
  39.0 2.3 %shard_map.89 = (bf16[512,1024]{1,0:T(8,128)(2,1)}, bf16[512,32]{1,0:T(8,128)(2,1)S(1)}) custom-call(s32[1]{0:T(128)} %bitcast.me_ref, s32[44,32]{1,0:T(8,128)S(1)} %add_bitcast_fusion.table_ref, bf16[32,1024]{1,0:T(8,128)(2,1)S(1)} %copy-done.4, bf16[32,512]{1,0:T(8,128)(2,1)S(1)} %shard_map.88.own_ref, bf16[32,512]{1,0:T(8,128)(2,1)S(1)} %collective-permute-done.1.other_ref), custom_call_target="tpu_custom_call" | custom-call | bytes 273416 | tf_op jit(solution)/shard_map/pallas_call | solution.py:26
  41.3 0.0 copy-start.2
  41.3 0.0 copy-start.3
  41.3 13.3 %all-to-all-start.1 = ((bf16[64,8,1024]{2,1,0:T(8,128)(2,1)}), bf16[64,8,1024]{2,1,0:T(8,128)(2,1)S(1)}, u32[]{:S(2)}, u32[]{:S(2)}) async-start(bf16[64,8,1024]{2,1,0:T(8,128)(2,1)} %bitcast.9), calls=%async_computation.1 | async-start | bytes 2097152 | tf_op jit(solution)/shard_map/all_to_all | solution.py:209
  54.7 0.0 copy-done.2
  54.7 0.0 copy-done.3
  54.7 0.2 shard_map.90
  54.9 2.5 %collective-permute-start.2 = (bf16[2048,128]{1,0:T(8,128)(2,1)S(1)}, bf16[2048,128]{1,0:T(8,128)(2,1)S(1)}, u32[]{:S(2)}, u32[]{:S(2)}) collective-permute-start(bf16[2048,128]{1,0:T(8,128)(2,1)S(1)} %get-tuple-element.21), channel_id=1, source_target_pairs={{0,1},{1,0},{2,3},{3,2},{4,5},{5,4},{6,7},{7,6},{8,9},{9,8},{10,11... | collective-permute-start | bytes 1572872 | tf_op jit(solution)/shard_map/ppermute | solution.py:220
  57.4 2.2 %collective-permute-start.3 = (bf16[2048,128]{1,0:T(8,128)(2,1)S(1)}, bf16[2048,128]{1,0:T(8,128)(2,1)S(1)}, u32[]{:S(2)}, u32[]{:S(2)}) collective-permute-start(bf16[2048,128]{1,0:T(8,128)(2,1)S(1)} %get-tuple-element.22), channel_id=1, source_target_pairs={{0,14},{1,3},{2,0},{3,5},{4,2},{5,7},{6,4},{7,9},{8,6},{9,11},{10,... | collective-permute-start | bytes 1572872 | tf_op jit(solution)/shard_map/ppermute | solution.py:220
  59.6 3.3 %collective-permute-start.4 = (bf16[2048,128]{1,0:T(8,128)(2,1)S(1)}, bf16[2048,128]{1,0:T(8,128)(2,1)S(1)}, u32[]{:S(2)}, u32[]{:S(2)}) collective-permute-start(bf16[2048,128]{1,0:T(8,128)(2,1)S(1)} %get-tuple-element.23), channel_id=1, source_target_pairs={{0,15},{1,2},{2,1},{3,4},{4,3},{5,6},{6,5},{7,8},{8,7},{9,10},{10,... | collective-permute-start | bytes 1572872 | tf_op jit(solution)/shard_map/ppermute | solution.py:220
  62.9 0.0 collective-permute-done.2.refs_0_
  62.9 5.9 %collective-permute-done.3.refs_1_ = bf16[2048,128]{1,0:T(8,128)(2,1)S(1)} collective-permute-done((bf16[2048,128]{1,0:T(8,128)(2,1)S(1)}, bf16[2048,128]{1,0:T(8,128)(2,1)S(1)}, u32[]{:S(2)}, u32[]{:S(2)}) %collective-permute-start.3) | collective-permute-done | bytes 524320 | tf_op jit(solution)/shard_map/ppermute | solution.py:220
  68.8 4.9 %collective-permute-done.4.refs_2_ = bf16[2048,128]{1,0:T(8,128)(2,1)S(1)} collective-permute-done((bf16[2048,128]{1,0:T(8,128)(2,1)S(1)}, bf16[2048,128]{1,0:T(8,128)(2,1)S(1)}, u32[]{:S(2)}, u32[]{:S(2)}) %collective-permute-start.4) | collective-permute-done | bytes 524320 | tf_op jit(solution)/shard_map/ppermute | solution.py:220
  73.7 8.0 %all-to-all-done.1 = bf16[64,8,1024]{2,1,0:T(8,128)(2,1)S(1)} async-done(((bf16[64,8,1024]{2,1,0:T(8,128)(2,1)}), bf16[64,8,1024]{2,1,0:T(8,128)(2,1)S(1)}, u32[]{:S(2)}, u32[]{:S(2)}) %all-to-all-start.1) | async-done | bytes 1048608 | tf_op jit(solution)/shard_map/all_to_all | solution.py:209
  81.7 4.3 %shard_map.91 = (bf16[512,512]{1,0:T(8,128)(2,1)}, bf16[1024,128]{1,0:T(8,128)(2,1)S(1)}, bf16[1024,128]{1,0:T(8,128)(2,1)S(1)}, bf16[1024,128]{1,0:T(8,128)(2,1)S(1)}, bf16[1024,128]{1,0:T(8,128)(2,1)S(1)}) custom-call(s32[1]{0:T(128)} %bitcast.me_ref, bf16[512,1024]{1,0:T(8,128)(2,1)S(1)} %bitcast.8, bf16[4,1024,128]{2,1,0:T(8,128)(2,1)} %up_hbm.1, ...), custom_call_target="tpu_custom_call" | custom-call | flops 2147483648 | bytes 9437192 | tf_op jit(solution)/shard_map/pallas_call | solution.py:26
  86.0 0.0 copy-start.6
  86.1 0.7 copy-done.6
  86.8 8.9 %all-to-all-start.2 = ((bf16[64,8,512]{2,1,0:T(8,128)(2,1)}), bf16[64,8,512]{2,1,0:T(8,128)(2,1)S(1)}, u32[]{:S(2)}, u32[]{:S(2)}) async-start(bf16[64,8,512]{2,1,0:T(8,128)(2,1)} %bitcast.4), calls=%async_computation.2 | async-start | bytes 1048576 | tf_op jit(solution)/shard_map/all_to_all | solution.py:209
  95.6 0.0 copy-done.7
  95.6 3.4 %collective-permute-start.5 = (bf16[1024,128]{1,0:T(8,128)(2,1)S(1)}, bf16[1024,128]{1,0:T(8,128)(2,1)S(1)}, u32[]{:S(2)}, u32[]{:S(2)}) collective-permute-start(bf16[1024,128]{1,0:T(8,128)(2,1)S(1)} %copy-done.7), channel_id=1, source_target_pairs={{1,0},{0,1},{3,2},{2,3},{5,4},{4,5},{7,6},{6,7},{9,8},{8,9},{11,10... | collective-permute-start | bytes 786440 | tf_op jit(solution)/shard_map/ppermute | solution.py:220
  99.1 1.9 %collective-permute-start.6 = (bf16[1024,128]{1,0:T(8,128)(2,1)S(1)}, bf16[1024,128]{1,0:T(8,128)(2,1)S(1)}, u32[]{:S(2)}, u32[]{:S(2)}) collective-permute-start(bf16[1024,128]{1,0:T(8,128)(2,1)S(1)} %get-tuple-element.27), channel_id=1, source_target_pairs={{14,0},{3,1},{0,2},{5,3},{2,4},{7,5},{4,6},{9,7},{6,8},{11,9},{8,1... | collective-permute-start | bytes 786440 | tf_op jit(solution)/shard_map/ppermute | solution.py:220
  101.0 2.1 %collective-permute-start.7 = (bf16[1024,128]{1,0:T(8,128)(2,1)S(1)}, bf16[1024,128]{1,0:T(8,128)(2,1)S(1)}, u32[]{:S(2)}, u32[]{:S(2)}) collective-permute-start(bf16[1024,128]{1,0:T(8,128)(2,1)S(1)} %get-tuple-element.28), channel_id=1, source_target_pairs={{15,0},{2,1},{1,2},{4,3},{3,4},{6,5},{5,6},{8,7},{7,8},{10,9},{9,1... | collective-permute-start | bytes 786440 | tf_op jit(solution)/shard_map/ppermute | solution.py:220
  103.1 0.1 copy.9.gate_ref
  103.2 0.0 collective-permute-done.5.refs_1_
  103.2 3.5 %collective-permute-done.6.refs_2_ = bf16[1024,128]{1,0:T(8,128)(2,1)S(1)} collective-permute-done((bf16[1024,128]{1,0:T(8,128)(2,1)S(1)}, bf16[1024,128]{1,0:T(8,128)(2,1)S(1)}, u32[]{:S(2)}, u32[]{:S(2)}) %collective-permute-start.6) | collective-permute-done | bytes 262176 | tf_op jit(solution)/shard_map/ppermute | solution.py:220
  106.7 2.6 %collective-permute-done.7.refs_3_ = bf16[1024,128]{1,0:T(8,128)(2,1)S(1)} collective-permute-done((bf16[1024,128]{1,0:T(8,128)(2,1)S(1)}, bf16[1024,128]{1,0:T(8,128)(2,1)S(1)}, u32[]{:S(2)}, u32[]{:S(2)}) %collective-permute-start.7) | collective-permute-done | bytes 262176 | tf_op jit(solution)/shard_map/ppermute | solution.py:220
  109.3 1.0 shard_map.92
  110.3 1.2 all-to-all-done.2
  111.6 0.3 shard_map.93
  111.9 6.2 %collective-permute-start.8 = (bf16[32,512]{1,0:T(8,128)(2,1)S(1)}, bf16[32,512]{1,0:T(8,128)(2,1)S(1)}, u32[]{:S(2)}, u32[]{:S(2)}) collective-permute-start(bf16[32,512]{1,0:T(8,128)(2,1)S(1)} %get-tuple-element.32), channel_id=1, source_target_pairs={{0,1},{1,0},{2,3},{3,2},{4,5},{5,4},{6,7},{7,6},{8,9},{9,8},{10,11... | collective-permute-start | bytes 98312 | tf_op jit(solution)/shard_map/ppermute | solution.py:220
  118.1 0.8 collective-permute-done.8.got_ref
  118.9 14.9 %all_to_all.21.i_ref = bf16[8,32,512]{2,1,0:T(8,128)(2,1)S(1)} all-to-all(bf16[8,32,512]{2,1,0:T(8,128)(2,1)S(1)} %shard_map.94), channel_id=1, replica_groups=mesh['expert'=64,'z'=8,'core'=2] {'z'}, dimensions={0} | all-to-all | bytes 524288 | tf_op jit(solution)/shard_map/all_to_all | solution.py:226
  133.9 2.4 %collective-permute-start.9 = (bf16[32,512]{1,0:T(8,128)(2,1)S(1)}, bf16[32,512]{1,0:T(8,128)(2,1)S(1)}, u32[]{:S(2)}, u32[]{:S(2)}) collective-permute-start(bf16[32,512]{1,0:T(8,128)(2,1)S(1)} %shard_map.95.own_ref), channel_id=1, source_target_pairs={{0,1},{1,0},{2,3},{3,2},{4,5},{5,4},{6,7},{7,6},{8,9},{9,8},{10,11... | collective-permute-start | bytes 98312 | tf_op jit(solution)/shard_map/ppermute | solution.py:220
  136.3 0.8 collective-permute-done.9.other_ref
  137.1 0.0 copy-done.1
  137.1 0.8 shard_map.96
  (11 shorter events, 0.1 us)
Async XLA Ops:
  0.6 0.7 copy-start.5
  1.3 1.0 copy-start
  2.7 16.9 %collective-permute-start = (bf16[32,512]{1,0:T(8,128)(2,1)S(1)}, bf16[32,512]{1,0:T(8,128)(2,1)S(1)}, u32[]{:S(2)}, u32[]{:S(2)}) collective-permute-start(bf16[32,512]{1,0:T(8,128)(2,1)S(1)} %get-tuple-element.19), channel_id=1, source_target_pairs={{0,1},{1,0},{2,3},{3,2},{4,5},{5,4},{6,7},{7,6},{8,9},{9,8},{10,11... | collective-permute-start | bytes 98312 | tf_op jit(solution)/shard_map/ppermute | solution.py:220
  34.4 3.7 %copy-start.8 = (s32[32,22]{0,1:T(8,128)S(1)}, s32[32,22]{0,1:T(8,128)}, u32[]{:S(2)}) copy-start(s32[32,22]{0,1:T(8,128)} %param.9) | copy-start | bytes 8452
  34.4 3.8 %copy-start.9 = (s32[32,22]{0,1:T(8,128)S(1)}, s32[32,22]{0,1:T(8,128)}, u32[]{:S(2)}) copy-start(s32[32,22]{0,1:T(8,128)} %param.8) | copy-start | bytes 8452
  34.4 4.6 %copy-start.4 = (bf16[32,1024]{1,0:T(8,128)(2,1)S(1)}, bf16[32,1024]{1,0:T(8,128)(2,1)}, u32[]{:S(2)}) copy-start(bf16[32,1024]{1,0:T(8,128)(2,1)} %latent_ref.1) | copy-start | bytes 196612
  34.5 4.5 %collective-permute-start.1 = (bf16[32,512]{1,0:T(8,128)(2,1)S(1)}, bf16[32,512]{1,0:T(8,128)(2,1)S(1)}, u32[]{:S(2)}, u32[]{:S(2)}) collective-permute-start(bf16[32,512]{1,0:T(8,128)(2,1)S(1)} %shard_map.88.own_ref), channel_id=1, source_target_pairs={{0,1},{1,0},{2,3},{3,2},{4,5},{5,4},{6,7},{7,6},{8,9},{9,8},{10,11... | collective-permute-start | bytes 98312 | tf_op jit(solution)/shard_map/ppermute | solution.py:220
  41.3 13.4 %copy-start.2 = (bf16[4,1024,128]{2,1,0:T(8,128)(2,1)S(1)}, bf16[4,1024,128]{2,1,0:T(8,128)(2,1)}, u32[]{:S(2)}) copy-start(bf16[4,1024,128]{2,1,0:T(8,128)(2,1)} %up_hbm.1) | copy-start | bytes 3145732
  41.3 13.4 %copy-start.3 = (bf16[4,128,1024]{2,1,0:T(8,128)(2,1)S(1)}, bf16[4,128,1024]{2,1,0:T(8,128)(2,1)}, u32[]{:S(2)}) copy-start(bf16[4,128,1024]{2,1,0:T(8,128)(2,1)} %down_hbm.1) | copy-start | bytes 3145732
  41.3 40.4 %all-to-all-start.1 = ((bf16[64,8,1024]{2,1,0:T(8,128)(2,1)}), bf16[64,8,1024]{2,1,0:T(8,128)(2,1)S(1)}, u32[]{:S(2)}, u32[]{:S(2)}) async-start(bf16[64,8,1024]{2,1,0:T(8,128)(2,1)} %bitcast.9), calls=%async_computation.1 | async-start | bytes 2097152 | tf_op jit(solution)/shard_map/all_to_all | solution.py:209
  54.9 8.0 %collective-permute-start.2 = (bf16[2048,128]{1,0:T(8,128)(2,1)S(1)}, bf16[2048,128]{1,0:T(8,128)(2,1)S(1)}, u32[]{:S(2)}, u32[]{:S(2)}) collective-permute-start(bf16[2048,128]{1,0:T(8,128)(2,1)S(1)} %get-tuple-element.21), channel_id=1, source_target_pairs={{0,1},{1,0},{2,3},{3,2},{4,5},{5,4},{6,7},{7,6},{8,9},{9,8},{10,11... | collective-permute-start | bytes 1572872 | tf_op jit(solution)/shard_map/ppermute | solution.py:220
  57.4 11.4 %collective-permute-start.3 = (bf16[2048,128]{1,0:T(8,128)(2,1)S(1)}, bf16[2048,128]{1,0:T(8,128)(2,1)S(1)}, u32[]{:S(2)}, u32[]{:S(2)}) collective-permute-start(bf16[2048,128]{1,0:T(8,128)(2,1)S(1)} %get-tuple-element.22), channel_id=1, source_target_pairs={{0,14},{1,3},{2,0},{3,5},{4,2},{5,7},{6,4},{7,9},{8,6},{9,11},{10,... | collective-permute-start | bytes 1572872 | tf_op jit(solution)/shard_map/ppermute | solution.py:220
  59.6 14.1 %collective-permute-start.4 = (bf16[2048,128]{1,0:T(8,128)(2,1)S(1)}, bf16[2048,128]{1,0:T(8,128)(2,1)S(1)}, u32[]{:S(2)}, u32[]{:S(2)}) collective-permute-start(bf16[2048,128]{1,0:T(8,128)(2,1)S(1)} %get-tuple-element.23), channel_id=1, source_target_pairs={{0,15},{1,2},{2,1},{3,4},{4,3},{5,6},{6,5},{7,8},{8,7},{9,10},{10,... | collective-permute-start | bytes 1572872 | tf_op jit(solution)/shard_map/ppermute | solution.py:220
  86.0 0.7 copy-start.6
  86.8 8.9 %copy-start.7 = (bf16[1024,128]{1,0:T(8,128)(2,1)S(1)}, bf16[1024,128]{1,0:T(8,128)(2,1)}, u32[]{:S(2)}) copy-start(bf16[1024,128]{1,0:T(8,128)(2,1)} %copy-done.6) | copy-start | bytes 786436
  86.8 24.8 %all-to-all-start.2 = ((bf16[64,8,512]{2,1,0:T(8,128)(2,1)}), bf16[64,8,512]{2,1,0:T(8,128)(2,1)S(1)}, u32[]{:S(2)}, u32[]{:S(2)}) async-start(bf16[64,8,512]{2,1,0:T(8,128)(2,1)} %bitcast.4), calls=%async_computation.2 | async-start | bytes 1048576 | tf_op jit(solution)/shard_map/all_to_all | solution.py:209
  95.6 7.6 %collective-permute-start.5 = (bf16[1024,128]{1,0:T(8,128)(2,1)S(1)}, bf16[1024,128]{1,0:T(8,128)(2,1)S(1)}, u32[]{:S(2)}, u32[]{:S(2)}) collective-permute-start(bf16[1024,128]{1,0:T(8,128)(2,1)S(1)} %copy-done.7), channel_id=1, source_target_pairs={{1,0},{0,1},{3,2},{2,3},{5,4},{4,5},{7,6},{6,7},{9,8},{8,9},{11,10... | collective-permute-start | bytes 786440 | tf_op jit(solution)/shard_map/ppermute | solution.py:220
  99.1 7.6 %collective-permute-start.6 = (bf16[1024,128]{1,0:T(8,128)(2,1)S(1)}, bf16[1024,128]{1,0:T(8,128)(2,1)S(1)}, u32[]{:S(2)}, u32[]{:S(2)}) collective-permute-start(bf16[1024,128]{1,0:T(8,128)(2,1)S(1)} %get-tuple-element.27), channel_id=1, source_target_pairs={{14,0},{3,1},{0,2},{5,3},{2,4},{7,5},{4,6},{9,7},{6,8},{11,9},{8,1... | collective-permute-start | bytes 786440 | tf_op jit(solution)/shard_map/ppermute | solution.py:220
  101.0 8.3 %collective-permute-start.7 = (bf16[1024,128]{1,0:T(8,128)(2,1)S(1)}, bf16[1024,128]{1,0:T(8,128)(2,1)S(1)}, u32[]{:S(2)}, u32[]{:S(2)}) collective-permute-start(bf16[1024,128]{1,0:T(8,128)(2,1)S(1)} %get-tuple-element.28), channel_id=1, source_target_pairs={{15,0},{2,1},{1,2},{4,3},{3,4},{6,5},{5,6},{8,7},{7,8},{10,9},{9,1... | collective-permute-start | bytes 786440 | tf_op jit(solution)/shard_map/ppermute | solution.py:220
  111.9 7.0 %collective-permute-start.8 = (bf16[32,512]{1,0:T(8,128)(2,1)S(1)}, bf16[32,512]{1,0:T(8,128)(2,1)S(1)}, u32[]{:S(2)}, u32[]{:S(2)}) collective-permute-start(bf16[32,512]{1,0:T(8,128)(2,1)S(1)} %get-tuple-element.32), channel_id=1, source_target_pairs={{0,1},{1,0},{2,3},{3,2},{4,5},{5,4},{6,7},{7,6},{8,9},{9,8},{10,11... | collective-permute-start | bytes 98312 | tf_op jit(solution)/shard_map/ppermute | solution.py:220
  118.9 18.2 %copy-start.1 = (bf16[1024,256]{1,0:T(8,128)(2,1)S(1)}, bf16[1024,256]{1,0:T(8,128)(2,1)}, u32[]{:S(2)}) copy-start(bf16[1024,256]{1,0:T(8,128)(2,1)} %out_w_ref.1) | copy-start | bytes 1572868
  133.9 3.2 %collective-permute-start.9 = (bf16[32,512]{1,0:T(8,128)(2,1)S(1)}, bf16[32,512]{1,0:T(8,128)(2,1)S(1)}, u32[]{:S(2)}, u32[]{:S(2)}) collective-permute-start(bf16[32,512]{1,0:T(8,128)(2,1)S(1)} %shard_map.95.own_ref), channel_id=1, source_target_pairs={{0,1},{1,0},{2,3},{3,2},{4,5},{5,4},{6,7},{7,6},{8,9},{9,8},{10,11... | collective-permute-start | bytes 98312 | tf_op jit(solution)/shard_map/ppermute | solution.py:220
